TPU v7x, 256 devices: a whole 4x4x8 slice. The times are simulated.
256 devices in a mesh: section: 32 (over y, z), tensor: 8 (over x, core).
Axes of the slice: x: 4, y: 4, z: 8, core: 2. Of those that a mesh axis runs over, the one named last changes fastest.
Arguments:
- pending_activations: bfloat16 [4096, 4096], P('section', 'tensor'), may hold values from -6 to 6
- embedded_segments: bfloat16 [256, 4096], P(None, 'tensor'), may hold values from -6 to 6
- asking_mapping_matrix: bfloat16 [32, 4096, 4096], P('section', None, 'tensor'), may hold values from -0.09375 to 0.09375
- pair_mapping_matrix: bfloat16 [32, 4096, 2048], P('section', None, 'tensor'), may hold values from -0.09375 to 0.09375
- attention_exit_matrix: bfloat16 [32, 4096, 4096], P('section', 'tensor'), may hold values from -0.375 to 0.375
- memo_pair_table: bfloat16 [32, 3968, 2048], P('section', None, 'tensor'), may hold values from -3.5 to 3.5
- entry_rmsnorm_scale: float32 [32, 4096], P('section'), may hold values from 0.5 to 1.5
- asking_rmsnorm_scale: float32 [32, 128], P('section'), may hold values from 0.5 to 1.5
- lookup_rmsnorm_scale: float32 [32, 128], P('section'), may hold values from 0.5 to 1.5
- deepstack_visual_features: bfloat16 [384, 3, 4096], P('section', None, 'tensor'), may hold values from -6 to 6
- visual_feature_positions: int32 [384], P('section'), may hold values from 0 to 511, as said below
Outputs:
- hidden_out: bfloat16 [4096, 4096], P('section', 'tensor')
- kv_appended: bfloat16 [32, 256, 2048], P('section', None, 'tensor')
Inputs may be any that keep to these rules, and one draw needn't show every extreme that they name: `visual_feature_positions`: distinct positions of the window of 512 rows that layers below 3 receive.
All inputs are finite; a program needn't handle non-finite values.
Results may differ from a plain program's by a relative error of at most 0.025.
Values may be sent and summed in bfloat16 or wider, within the bound.
A program may use at most 128 MiB of HBM per device.

v0:
```python
import jax
import jax.numpy as jnp
from jax import lax
from jax.sharding import PartitionSpec as P

epsilon = 1e-06
rope_theta = 5000000.0


def from_behind(value, axis, by):
    length = lax.axis_size(axis)
    pairs = [(i, i + by) for i in range(length) if 0 <= i + by < length]
    return lax.ppermute(value, axis, pairs)


def rotary(values, position):
    head_width = values.shape[-1]
    half_width = head_width // 2
    frequency = rope_theta ** (-(jnp.arange(half_width, dtype=jnp.float32) * 2.0 / head_width))
    angles = position.astype(jnp.float32)[:, None] * frequency[None, :]
    cos_part = jnp.cos(angles)[:, None, :]
    sin_part = jnp.sin(angles)[:, None, :]
    lower_half = values[..., :half_width]
    upper_half = values[..., half_width:]
    return jnp.concatenate(
        [
            lower_half * cos_part - upper_half * sin_part,
            upper_half * cos_part + lower_half * sin_part,
        ],
        axis=-1,
    )


def rms_scale(values, gain):
    return values * lax.rsqrt(jnp.mean(values * values, axis=-1, keepdims=True) + epsilon) * gain


def attention(query, keys, values, valid):
    scores = jnp.einsum(
        "ckgh,pkh->kgcp", query, keys, preferred_element_type=jnp.float32
    ) * query.shape[-1] ** (-0.5)
    weights = jnp.where(valid[None, None], jnp.exp(scores), 0.0)
    total = jnp.sum(weights, axis=-1)
    summed = jnp.einsum(
        "kgcp,pkh->ckgh", weights.astype(jnp.bfloat16), values, preferred_element_type=jnp.float32
    )
    return (summed / jnp.transpose(total, (2, 0, 1))[..., None]).astype(jnp.bfloat16)


def layer_core(
    full_rows,
    section_id,
    step_no,
    section_count,
    query_w,
    keyval_w,
    out_w,
    cached,
    in_gain,
    q_gain,
    k_gain,
    appended,
):
    bundle_count = full_rows.shape[0]
    head_width = q_gain.shape[0]
    local_kv = keyval_w.shape[1] // (2 * head_width)
    local_heads = query_w.shape[1] // head_width
    cap_len = cached.shape[0]
    rows_f = full_rows.astype(jnp.float32)
    normed = rms_scale(rows_f, in_gain).astype(jnp.bfloat16)
    query = jnp.dot(normed, query_w, preferred_element_type=jnp.float32)
    keyval = jnp.dot(normed, keyval_w, preferred_element_type=jnp.float32).reshape(
        bundle_count, local_kv, 2, head_width
    )
    offset = (section_count - 1 - section_id) * bundle_count
    position = offset + step_no * bundle_count + jnp.arange(bundle_count, dtype=jnp.int32)
    query = rotary(
        rms_scale(query.reshape(bundle_count, local_heads, head_width), q_gain), position
    )
    query = query.astype(jnp.bfloat16).reshape(
        bundle_count, local_kv, local_heads // local_kv, head_width
    )
    keys_new = rotary(rms_scale(keyval[:, :, 0], k_gain), position)
    fresh = jnp.stack([keys_new, keyval[:, :, 1]], axis=2).astype(jnp.bfloat16)
    appended = appended.at[step_no * bundle_count : (step_no + 1) * bundle_count].set(fresh)
    cached_heads = cached.reshape(cap_len, local_kv, 2, head_width)
    all_keys = jnp.concatenate([cached_heads[:, :, 0], appended[:, :, 0]], axis=0)
    all_values = jnp.concatenate([cached_heads[:, :, 1], appended[:, :, 1]], axis=0)
    cache_valid = jnp.broadcast_to(
        jnp.arange(cap_len, dtype=jnp.int32)[None, :] < offset, (bundle_count, cap_len)
    )
    fresh_valid = (
        jnp.arange(appended.shape[0], dtype=jnp.int32)[None, :]
        <= step_no * bundle_count + jnp.arange(bundle_count, dtype=jnp.int32)[:, None]
    )
    valid = jnp.concatenate([cache_valid, fresh_valid], axis=1)
    attended = attention(query, all_keys, all_values, valid).reshape(
        bundle_count, local_heads * head_width
    )
    return (jnp.dot(attended, out_w, preferred_element_type=jnp.float32), appended)


def visual_term(chosen, places_all, section_id, step_no, bundle_count, levels_count):
    window = step_no + levels_count - 1 - section_id
    targets = window * bundle_count + jnp.arange(bundle_count, dtype=jnp.int32)
    onehot = ((places_all[None, :] == targets[:, None]) & (section_id < levels_count)).astype(
        jnp.bfloat16
    )
    return jnp.dot(onehot, chosen, preferred_element_type=jnp.float32)


def body(
    pending_activations,
    embedded_segments,
    asking_mapping_matrix,
    pair_mapping_matrix,
    attention_exit_matrix,
    memo_pair_table,
    entry_rmsnorm_scale,
    asking_rmsnorm_scale,
    lookup_rmsnorm_scale,
    deepstack_visual_features,
    visual_feature_positions,
):
    section_id = lax.axis_index("section")
    section_count = lax.axis_size("section")
    bundle_count = pending_activations.shape[0]
    portion_breadth = pending_activations.shape[1]
    column_start = lax.axis_index("tensor") * portion_breadth
    steps_total = embedded_segments.shape[0] // bundle_count
    head_width = asking_rmsnorm_scale.shape[1]
    local_kv = pair_mapping_matrix.shape[2] // (2 * head_width)
    levels_count = deepstack_visual_features.shape[1]
    table_all, places_all = (
        lax.all_gather(deepstack_visual_features, "section", axis=0, tiled=True),
        lax.all_gather(visual_feature_positions, "section", axis=0, tiled=True),
    )
    chosen = lax.dynamic_index_in_dim(
        table_all, jnp.minimum(section_id, levels_count - 1), 1, keepdims=False
    )
    query_w = asking_mapping_matrix[0]
    keyval_w = pair_mapping_matrix[0]
    out_w = attention_exit_matrix[0]
    cached = memo_pair_table[0]
    in_gain = entry_rmsnorm_scale[0]
    q_gain = asking_rmsnorm_scale[0]
    k_gain = lookup_rmsnorm_scale[0]
    appended = jnp.zeros((steps_total * bundle_count, local_kv, 2, head_width), jnp.bfloat16)
    held_full, arrive_full = (
        lax.all_gather(pending_activations, "tensor", axis=1, tiled=True),
        lax.all_gather(embedded_segments, "tensor", axis=1, tiled=True),
    )
    full_width = held_full.shape[1]
    previous = held_full
    for step_no in range(steps_total):
        moved = from_behind(previous, "section", 1)
        incoming = arrive_full[step_no * bundle_count : (step_no + 1) * bundle_count]
        current = jnp.where(section_id == 0, incoming, moved)
        partial_sum, appended = layer_core(
            current,
            section_id,
            step_no,
            section_count,
            query_w,
            keyval_w,
            out_w,
            cached,
            in_gain,
            q_gain,
            k_gain,
            appended,
        )
        injected = visual_term(chosen, places_all, section_id, step_no, bundle_count, levels_count)
        placed = lax.dynamic_update_slice(
            jnp.zeros((bundle_count, full_width), jnp.float32), injected, (0, column_start)
        )
        summed = lax.psum((partial_sum + placed).astype(jnp.bfloat16), "tensor").astype(jnp.float32)
        previous = (current.astype(jnp.float32) + summed).astype(jnp.bfloat16)
    hidden_out = lax.dynamic_slice_in_dim(previous, column_start, portion_breadth, 1)
    kv_appended = appended.reshape(1, steps_total * bundle_count, local_kv * 2 * head_width)
    return (hidden_out, kv_appended)


def solution(mesh):
    return jax.shard_map(
        body,
        mesh=mesh,
        in_specs=(
            P("section", "tensor"),
            P(None, "tensor"),
            P("section", None, "tensor"),
            P("section", None, "tensor"),
            P("section", "tensor", None),
            P("section", None, "tensor"),
            P("section", None),
            P("section", None),
            P("section", None),
            P("section", None, "tensor"),
            P("section"),
        ),
        out_specs=(P("section", "tensor"), P("section", None, "tensor")),
        check_vma=False,
    )
```

profile of v0, /device:TPU:8, one launch (start us, length us, event | category | flops | bytes accessed | tf_op | source)
XLA Modules:
  0.0 348.0 jit_solution(9361434258681965641)
XLA Ops:
  9.4 2.9 copy.63
  12.4 6.9 %copy.64 = bf16[512,4096]{1,0:T(8,128)(2,1)} copy(bf16[512,4096]{0,1:T(8,128)(2,1)} %bitcast.152) | data formatting | bytes 8388608 | tf_op jit(solution)/shard_map/dot_general | solution.py:71
  19.3 4.1 %copy.44 = bf16[1,3968,256]{1,2,0:T(8,128)(2,1)} copy(bf16[1,3968,256]{2,1,0:T(8,128)(2,1)} %param.20) | data formatting | bytes 4063232 | tf_op args[5]
  23.3 2.7 slice_bitcast_fusion
  28.9 22.3 %all-reduce.1 = s32[384]{0:T(512)S(1)} all-reduce(s32[384]{0:T(512)S(1)} %dynamic-update-slice.8), channel_id=1, replica_groups=mesh['section'=32,'tensor'=8] {'section'}, use_global_device_ids=true, to_apply=%add.1 | all-reduce | flops 384 | bytes 3072
  51.7 2.9 collective-permute-start
  54.6 4.7 %pad_add_fusion.1 = (pred[128,4224]{0,1:T(8,128)(4,1)}, pred[128,4224]{0,1:T(8,128)(4,1)}) fusion(pred[128,256]{0,1:T(8,128)(4,1)S(1)} %get-tuple-element.62, pred[4224]{0:T(1024)(128)(4,1)S(1)} %pad.25.clone, pred[128,256]{0,1:T(8,128)(4,1)S(1)} %get-tuple-element.63), kind=kLoop, calls=%fused_computation.16 | loop fusion | flops 1081344 | bytes 1151104 | tf_op jit(solution)/shard_map/concatenate | solution.py:96
  59.3 58.2 %all-gather.8.cloned.1.call-done = bf16[384,3,512]{2,1,0:T(4,128)(2,1)} async-done(((bf16[12,3,512]{2,1,0:T(4,128)(2,1)}), bf16[384,3,512]{2,1,0:T(4,128)(2,1)}) %all-gather.8.cloned.1.call-update) | async-done | bytes 1179664 | tf_op jit(solution)/shard_map/all_gather | solution.py:135
  117.5 3.1 constant_dynamic-slice_fusion
  121.6 24.1 %all-gather.4.cloned.1.call-done = bf16[256,4096]{1,0:T(8,128)(2,1)} async-done(((bf16[256,512]{1,0:T(8,128)(2,1)}), bf16[256,4096]{1,0:T(8,128)(2,1)}) %all-gather.4.cloned.1.call-update) | async-done | bytes 2097168 | tf_op jit(solution)/shard_map/all_gather | solution.py:151
  145.7 2.0 fusion.10
  149.1 3.6 %multiply_reduce_fusion.2 = (f32[128,4]{0,1:T(4,128)S(1)}, f32[128,4,128]{0,2,1:T(8,128)S(1)}) fusion(bf16[4,128,4096]{2,1,0:T(8,128)(2,1)} %bitcast.147, bf16[128,4096]{1,0:T(8,128)(2,1)S(1)} %get-tuple-element.29, f32[4096]{0:T(1024)S(1)} %bitcast.161, f32[128]{0:T(128)S(1)} %add_rsqrt_fusion.5), kind=kOutput, calls=%fused_computation.60 | convolution fusion | flops 539098624 | bytes 5523968 | tf_op jit(solution)/shard_map/dot_general | solution.py:71
  152.9 3.0 fusion.90
  156.7 1.4 copy-done.1
  160.7 67.9 %all-reduce.5.cloned.1.call-done = bf16[128,4096]{1,0:T(8,128)(2,1)} async-done(((bf16[128,4096]{1,0:T(8,128)(2,1)}), bf16[128,4096]{1,0:T(8,128)(2,1)}) %all-reduce.5.cloned.1.call-update) | async-done | bytes 1048592 | tf_op jit(solution)/shard_map/psum | solution.py:177
  228.7 1.5 fusion.13
  230.1 3.6 %collective-permute-start.1 = (bf16[128,4096]{1,0:T(8,128)(2,1)S(1)}, bf16[128,4096]{1,0:T(8,128)(2,1)}, u32[]{:S(2)}, u32[]{:S(2)}) collective-permute-start(bf16[128,4096]{1,0:T(8,128)(2,1)S(1)} %fusion.13), channel_id=1, source_target_pairs={{0,8},{8,16},{16,24},{24,32},{32,40},{40,48},{48,56},{56,64},{64,7... | collective-permute-start | bytes 3145736 | tf_op jit(solution)/shard_map/ppermute | solution.py:13
  233.8 23.3 %collective-permute-done.1 = bf16[128,4096]{1,0:T(8,128)(2,1)} collective-permute-done((bf16[128,4096]{1,0:T(8,128)(2,1)S(1)}, bf16[128,4096]{1,0:T(8,128)(2,1)}, u32[]{:S(2)}, u32[]{:S(2)}) %collective-permute-start.1) | collective-permute-done | bytes 1048608 | tf_op jit(solution)/shard_map/ppermute | solution.py:13
  257.1 2.0 multiply_reduce_fusion
  261.3 1.4 multiply_reduce_fusion.1
  263.4 3.6 %fusion.91 = (f32[4,128]{1,0:T(4,128)S(1)}, bf16[1,4,128,4224]{2,3,1,0:T(8,128)(2,1)S(1)}) fusion(bf16[128,4,64]{0,2,1:T(8,128)(2,1)S(1)} %get-tuple-element.33, bf16[128,4,64]{0,2,1:T(8,128)(2,1)S(1)} %get-tuple-element.32, bf16[256,1,128]{2,0,1:T(8,128)(2,1)S(1)} %copy.53, bf16[3968,1,128]{2,0,1:T(8,128)(2,1)} %bitcast.155, ...), kind=kOutput, calls=%fused_computation.144 | convolution fusion | flops 564723200 | bytes 6080512 | tf_op jit(solution)/shard_map/ckgh,pkh->kgcp/dot_general | solution.py:39
  267.7 1.4 copy-done.2
  272.2 67.7 %all-reduce.7.cloned.1.call-done = bf16[128,4096]{1,0:T(8,128)(2,1)} async-done(((bf16[128,4096]{1,0:T(8,128)(2,1)}), bf16[128,4096]{1,0:T(8,128)(2,1)}) %all-reduce.7.cloned.1.call-update) | async-done | bytes 1048592 | tf_op jit(solution)/shard_map/psum | solution.py:177
  339.9 1.6 fusion.48
  (94 shorter events, 17.2 us)
Async XLA Ops:
  7.2 44.5 %all-gather.6.cloned.1.call-start = ((), (), s32[]{:S(2)}) async-start(), calls=%async_computation.1 | async-start | bytes 1179648 | tf_op jit(solution)/shard_map/all_gather | solution.py:150
  7.9 109.6 %all-gather.8.cloned.1.call-start = ((), (), s32[]{:S(2)}) async-start(), calls=%async_computation.2 | async-start | bytes 1622016 | tf_op jit(solution)/shard_map/all_gather | solution.py:135
  8.6 137.0 %all-gather.4.cloned.1.call-start = ((), (), s32[]{:S(2)}) async-start(), calls=%async_computation | async-start | bytes 2359296 | tf_op jit(solution)/shard_map/all_gather | solution.py:151
  9.4 219.3 %all-reduce.5.cloned.1.call-start = ((), (), s32[]{:S(2)}) async-start(), calls=%async_computation.3 | async-start | bytes 2097152 | tf_op jit(solution)/shard_map/psum | solution.py:177
  12.4 135.3 %copy-start.3 = (bf16[256,4096]{1,0:T(8,128)(2,1)}, bf16[256,4096]{1,0:T(8,128)(2,1)S(1)}, u32[]{:S(2)}) copy-start(bf16[256,4096]{1,0:T(8,128)(2,1)S(1)} %copy.63) | copy-start | bytes 6291460
  23.3 4.1 %copy-start.15 = (u32[256]{0:T(256)S(1)}, u32[256]{0:T(256)}, u32[]{:S(2)}) copy-start(u32[256]{0:T(256)} %constant.122) | copy-start | bytes 3076
  23.3 5.3 %copy-start.14 = (s32[12]{0:T(128)S(1)}, s32[12]{0:T(128)}, u32[]{:S(2)}) copy-start(s32[12]{0:T(128)} %param.25) | copy-start | bytes 148
  51.7 69.0 %collective-permute-start = (bf16[128,4096]{1,0:T(8,128)(2,1)}, bf16[128,4096]{1,0:T(8,128)(2,1)S(1)}, u32[]{:S(2)}, u32[]{:S(2)}) collective-permute-start(bf16[128,4096]{1,0:T(8,128)(2,1)} %all-gather.6.cloned.1.call-done), channel_id=1, source_target_pairs={{0,8},{8,16},{16,24},{24,32},{32,40},{40,48},{48,56},{56,64},{64,7... | collective-permute-start | bytes 3145736 | tf_op jit(solution)/shard_map/ppermute | solution.py:13
  59.3 88.4 %copy-start.11 = (f32[1,4096]{1,0:T(1,128)S(1)}, f32[1,4096]{1,0:T(1,128)}, u32[]{:S(2)}) copy-start(f32[1,4096]{1,0:T(1,128)} %param.21) | copy-start | bytes 49156
  120.6 1.0 copy-start.6
  147.7 0.9 copy-start.12
  149.1 3.7 %copy-start.13 = (f32[1,128]{1,0:T(1,128)S(1)}, f32[1,128]{1,0:T(1,128)}, u32[]{:S(2)}) copy-start(f32[1,128]{1,0:T(1,128)} %param.22) | copy-start | bytes 1540
  149.1 3.8 %copy-start.7 = (bf16[3968,1,1,128]{3,0,2,1:T(8,128)(2,1)S(1)}, bf16[3968,1,1,128]{3,0,2,1:T(8,128)(2,1)}, u32[]{:S(2)}) copy-start(bf16[3968,1,1,128]{3,0,2,1:T(8,128)(2,1)} %copy.65) | copy-start | bytes 3047428
  149.1 3.8 %copy-start.10 = (pred[128,4224]{0,1:T(8,128)(4,1)S(1)}, pred[128,4224]{0,1:T(8,128)(4,1)}, u32[]{:S(2)}) copy-start(pred[128,4224]{0,1:T(8,128)(4,1)} %get-tuple-element.45) | copy-start | bytes 1622020
  152.9 3.0 copy-start.8
  155.9 2.2 copy-start.1
  158.1 1.1 copy-start.5
  160.7 179.2 %all-reduce.7.cloned.1.call-start = ((), (), s32[]{:S(2)}) async-start(), calls=%async_computation.4 | async-start | bytes 2097152 | tf_op jit(solution)/shard_map/psum | solution.py:177
  230.1 27.0 %collective-permute-start.1 = (bf16[128,4096]{1,0:T(8,128)(2,1)S(1)}, bf16[128,4096]{1,0:T(8,128)(2,1)}, u32[]{:S(2)}, u32[]{:S(2)}) collective-permute-start(bf16[128,4096]{1,0:T(8,128)(2,1)S(1)} %fusion.13), channel_id=1, source_target_pairs={{0,8},{8,16},{16,24},{24,32},{32,40},{40,48},{48,56},{56,64},{64,7... | collective-permute-start | bytes 3145736 | tf_op jit(solution)/shard_map/ppermute | solution.py:13
  233.8 25.3 %copy-start.4 = (bf16[256,4096]{1,0:T(8,128)(2,1)S(1)}, bf16[256,4096]{1,0:T(8,128)(2,1)}, u32[]{:S(2)}) copy-start(bf16[256,4096]{1,0:T(8,128)(2,1)} %copy-done.3) | copy-start | bytes 6291460
  259.1 2.2 copy-start
  263.3 3.6 %copy-start.9 = (bf16[3968,1,128]{0,2,1:T(8,128)(2,1)S(1)}, bf16[3968,1,128]{0,2,1:T(8,128)(2,1)}, u32[]{:S(2)}) copy-start(bf16[3968,1,128]{0,2,1:T(8,128)(2,1)} %get-tuple-element.30) | copy-start | bytes 3047428
  266.9 2.2 copy-start.2
Sparse Core Ops, SparseCore 0:
  9.8 28.7 all-gather.5
  41.2 76.2 all-gather.7
  119.3 26.2 all-gather.3
  160.8 67.8 all-reduce.4
  271.4 68.3 all-reduce.6
where the time goes:
time: 349 us; the launch traced here: 348 us
  waiting for transfers between devices  243 us (70%)
  local copies, waits for them, and re-layouts  27.9 us (8%)
  blocking collectives  22.3 us (6%)
  matrix products  16.7 us (5%)
  other arithmetic  16.1 us (5%)
  between operations  15 us (4%)
  starting transfers between devices  6.76 us (2%)
    psum x2, waiting for transfers between devices, body(): lax.psum((partial_sum + placed).astype(jnp.bfloat16), 'tensor')  136 us
    all_gather x1, waiting for transfers between devices, body(): lax.all_gather(deepstack_visual_features, 'section', axis=0, tiled=True)  58.2 us
    all_gather x1, waiting for transfers between devices, body(): lax.all_gather(embedded_segments, 'tensor', axis=1, tiled=True)  24.1 us
    ppermute x2, waiting for transfers between devices, from_behind(): return lax.ppermute(value, axis, pairs)  23.3 us
    unnamed x1, blocking collectives  22.3 us
    unnamed x37, local copies, waits for them, and re-layouts  11.8 us
  transfers between devices with their start and end apart: 7, of which 5 were waited for; matrix products, arithmetic and copies ran while one was open for 8% of the time, Pallas kernels for 0%

commit v1 on v0

v1 whole, which is shorter than its diff:
```python
import functools
import math

import jax
import jax.numpy as jnp
from jax import lax
from jax.experimental import pallas as pl
from jax.experimental.pallas import tpu as pltpu
from jax.sharding import PartitionSpec as P

MESH = pl.DeviceIdType.MESH
EPS = 1e-06
THETA = 5000000.0
PAD = 16
F32 = jnp.float32
BF16 = jnp.bfloat16


def kernel(
    sections,
    pend,
    emb,
    wq_h,
    wkv_h,
    wo_h,
    memo,
    in_gain_h,
    q_gain_h,
    k_gain_h,
    feat_h,
    pos,
    out,
    kv_out,
    wqkv,
    wo,
    kv,
    in_gain,
    q_gain,
    k_gain,
    feat,
    msg,
    fbuf,
    inj,
    cs,
    sn,
    xb,
    ss,
    acc,
    qs,
    pv,
    att,
    sib_src,
    sib_dst,
    opp_src,
    rel_dst,
    nb_src,
    nb_dst,
    keep,
    yb,
    load_sem,
    emb_sem,
    fs_sem,
    fr_sem,
    ags,
    agr,
    rss,
    rsr,
    out_sem,
):
    S = sections
    steps, T, R, C = xb.shape
    half = R // 2
    HD = 128
    HC = att.shape[1]
    G = HC // HD
    D = T * C
    rows, levels = feat.shape[0], feat.shape[1]
    chunk = 4 * R
    s = lax.axis_index("section")
    me = lax.axis_index("tensor")
    x = me // 2
    c = me % 2
    ring = T // 2

    def block(step, parity):
        return 2 * ((x + step) % ring) + parity

    sib = block(0, 1 - c)
    right, left, opp = block(1, c), block(ring - 1, c), block(2, c)
    sright, sleft, sopp = block(1, 1 - c), block(ring - 1, 1 - c), block(2, 1 - c)
    off = pl.multiple_of((S - 1 - s) * R, R)

    ends = [
        (feat_h, feat),
        (in_gain_h, in_gain),
        (q_gain_h, q_gain),
        (k_gain_h, k_gain),
        (wq_h, wqkv.at[:, :, pl.ds(0, HC)]),
        (wkv_h, wqkv.at[:, :, pl.ds(HC, 2 * HD)]),
        (memo, kv.at[pl.ds(0, memo.shape[0])]),
    ] + [(wo_h.at[:, pl.ds(j * C, C)], wo.at[j]) for j in range(T)]

    def load(i):
        return pltpu.make_async_copy(*ends[i], load_sem.at[i])

    for i in range(7 + T):
        load(i).start()

    def enter(step):
        return pltpu.make_async_copy(
            emb.at[pl.ds(step * R, R)], xb.at[step, me], emb_sem.at[step]
        )

    @pl.when(s == 0)
    def _():
        for step in range(steps):
            enter(step).start()

    barrier = pltpu.get_barrier_semaphore()
    for peer in (sib, right, left):
        pl.semaphore_signal(barrier, inc=1, device_id={"tensor": peer}, device_id_type=MESH)

    @pl.when(s < levels)
    def _():
        def greet(k, carry):
            @pl.when(k != s)
            def _():
                pl.semaphore_signal(barrier, inc=1, device_id={"section": k}, device_id_type=MESH)

            return carry

        lax.fori_loop(0, S, greet, 0)

    @pl.when(s >= levels)
    def _():
        pl.semaphore_signal(barrier, inc=1, device_id={"section": s - 1}, device_id_type=MESH)

    peers = 3 + levels - jnp.where(s < levels, 1, 0)
    peers = peers + jnp.where((s >= levels - 1) & (s < S - 1), 1, 0)
    pl.semaphore_wait(barrier, peers)

    def shift(source, step, h):
        return pltpu.make_async_remote_copy(
            src_ref=source.at[pl.ds(h * half, half)],
            dst_ref=xb.at[step, me, pl.ds(h * half, half)],
            send_sem=ags.at[step, h],
            recv_sem=agr.at[step, h],
            device_id={"section": jnp.minimum(s + 1, S - 1)},
            device_id_type=MESH,
        )

    @pl.when(s < S - 1)
    def _():
        for h in range(2):
            shift(pend, 0, h).start()

    for i in range(4):
        load(i).wait()
    col = lax.broadcasted_iota(jnp.int32, (PAD, steps * R), 1)
    row = lax.broadcasted_iota(jnp.int32, (PAD, steps * R), 0)
    place = jnp.full((PAD, steps * R), -1000000, jnp.int32)
    for r in range(rows):
        place = jnp.where(row == r, pos[r], place)
    msg[...] = jnp.zeros_like(msg)
    everything = feat[...].astype(F32)
    for level in range(levels):
        msg[level, 0:rows, 0:C] = everything[:, level, :].astype(BF16)
        hit = place - (levels - 1 - level) * R == col
        msg[level, :, C:] = jnp.where(hit, 1.0, 0.0).astype(BF16)

    def feature(level):
        return pltpu.make_async_remote_copy(
            src_ref=msg.at[level],
            dst_ref=fbuf.at[pl.ds(s * PAD, PAD)],
            send_sem=fs_sem.at[level],
            recv_sem=fr_sem,
            device_id={"section": level},
            device_id_type=MESH,
        )

    for level in range(levels):

        @pl.when(s != level)
        def _():
            feature(level).start()

        @pl.when(s == level)
        def _():
            fbuf[pl.ds(pl.multiple_of(s * PAD, PAD), PAD), :] = msg[level]

    lane = lax.broadcasted_iota(jnp.int32, (R, HD), 1)
    fold = jnp.where(lane < HD // 2, lane, lane - HD // 2).astype(F32)
    frequency = jnp.exp(fold * (-2.0 * math.log(THETA) / HD))
    for step in range(steps):
        place = off + step * R + lax.broadcasted_iota(jnp.int32, (R, HD), 0)
        angle = place.astype(F32) * frequency
        cs[step] = jnp.cos(angle)
        sn[step] = jnp.where(lane < HD // 2, -jnp.sin(angle), jnp.sin(angle))
    tail = kv.shape[0] - memo.shape[0]
    kv[pl.ds(memo.shape[0], tail), :] = jnp.zeros((tail, 2 * HD), BF16)

    for i in (4, 5):
        load(i).wait()

    def step_body(t, carry):
        def piece(b, h):
            return xb.at[t, b, pl.ds(h * half, half)]

        def gather(slot_out, b, h, peer, slot_in):
            return pltpu.make_async_remote_copy(
                src_ref=piece(b, h),
                dst_ref=piece(b, h),
                send_sem=ags.at[t, slot_out],
                recv_sem=agr.at[t, slot_in],
                device_id={"tensor": peer},
                device_id_type=MESH,
            )

        sends = []

        def send(*args):
            copy = gather(len(sends) + 2, *args)
            copy.start()
            sends.append(copy)

        def arrived(slot, b, h):
            gather(0, b, h, sib, slot).wait_recv()

        def project(b):
            rows_f = xb[t, b].astype(F32)
            square = rows_f * rows_f
            total = square[:, 0:HD]
            for g in range(1, C // HD):
                total = total + square[:, g * HD : (g + 1) * HD]
            ss[...] += total
            gain = in_gain[:, pl.ds(pl.multiple_of(b * C, C), C)]
            acc[...] += jnp.dot(
                (rows_f * gain).astype(BF16), wqkv[b], preferred_element_type=F32
            )

        ss[...] = jnp.zeros_like(ss)
        acc[...] = jnp.zeros_like(acc)

        @pl.when(s == 0)
        def _():
            enter(t).wait()

        for h in range(2):

            @pl.when(s > 0)
            def _():
                arrived(h, me, h)

            send(me, h, right, 4 + h)
            send(me, h, left, 6 + h)
            send(me, h, sib, 2 + h)
        project(me)
        arrived(4, left, 0)
        send(left, 0, right, 12)
        send(left, 0, sib, 8)
        arrived(7, right, 1)
        send(right, 1, left, 13)
        send(right, 1, sib, 11)
        arrived(5, left, 1)
        send(left, 1, sib, 9)
        arrived(6, right, 0)
        send(right, 0, sib, 10)
        arrived(2, sib, 0)
        arrived(3, sib, 1)
        project(sib)
        project(left)
        project(right)
        arrived(12, opp, 0)
        send(opp, 0, sib, 14)
        arrived(13, opp, 1)
        send(opp, 1, sib, 15)
        project(opp)
        arrived(8, sleft, 0)
        arrived(9, sleft, 1)
        project(sleft)
        arrived(10, sright, 0)
        arrived(11, sright, 1)
        project(sright)
        arrived(14, sopp, 0)
        arrived(15, sopp, 1)
        project(sopp)

        scale = lax.rsqrt(jnp.sum(ss[...], axis=-1, keepdims=True) * (1.0 / D) + EPS)
        cos, sin = cs[t], sn[t]

        def head(value, gain):
            value = value * scale
            mean = jnp.sum(value * value, axis=-1, keepdims=True) * (1.0 / HD)
            value = value * lax.rsqrt(mean + EPS) * gain
            return value * cos + pltpu.roll(value, HD // 2, 1) * sin

        for g in range(G):
            query = head(acc[:, g * HD : (g + 1) * HD], q_gain[...])
            qs[g * R : (g + 1) * R, :] = (query * (math.log2(math.e) * HD**-0.5)).astype(BF16)

        @pl.when(t == 0)
        def _():
            load(6).wait()

        here = pl.ds(pl.multiple_of(off + t * R, R), R)
        kv[here, 0:HD] = head(acc[:, HC : HC + HD], k_gain[...]).astype(BF16)
        kv[here, HD:] = (acc[:, HC + HD :] * scale).astype(BF16)
        appended(t).start()

        pv[...] = jnp.zeros_like(pv)
        first = off + t * R
        whole = first // chunk

        def attend(at, masked):
            keys = kv[pl.ds(pl.multiple_of(at * chunk, chunk), chunk), :]
            values = jnp.concatenate([keys[:, HD:], jnp.ones((chunk, HD), BF16)], axis=1)
            for g in range(G):
                score = lax.dot_general(
                    qs[g * R : (g + 1) * R, :],
                    keys[:, 0:HD],
                    (((1,), (1,)), ((), ())),
                    preferred_element_type=F32,
                )
                weight = jnp.exp2(score)
                if masked:
                    slot = at * chunk + lax.broadcasted_iota(jnp.int32, (R, chunk), 1)
                    last = first + lax.broadcasted_iota(jnp.int32, (R, chunk), 0)
                    weight = jnp.where(slot <= last, weight, 0.0)
                pv[g * R : (g + 1) * R, :] += jnp.dot(
                    weight.astype(BF16), values, preferred_element_type=F32
                )

        def whole_chunk(at, carry):
            attend(at, False)
            return carry

        lax.fori_loop(0, whole, whole_chunk, 0)
        attend(whole, True)
        for g in range(G):
            found = pv[g * R : (g + 1) * R, :]
            att[:, g * HD : (g + 1) * HD] = (found[:, 0:HD] / found[:, HD:]).astype(BF16)

        @pl.when(t == 0)
        def _():
            for j in range(T):
                load(7 + j).wait()

        def part(b):
            return jnp.dot(att[...], wo[b], preferred_element_type=F32)

        def reduce(slot, source, target, peer):
            return pltpu.make_async_remote_copy(
                src_ref=source,
                dst_ref=target,
                send_sem=rss.at[t, slot],
                recv_sem=rsr.at[t, slot],
                device_id={"tensor": peer},
                device_id_type=MESH,
            )

        top, low = pl.ds(0, half), pl.ds(half, half)
        moves = [
            reduce(d, sib_src.at[t, d], sib_dst.at[t, d], sib) for d in range(4)
        ] + [
            reduce(4, opp_src.at[t, top], rel_dst.at[t, 0], right),
            reduce(5, opp_src.at[t, low], rel_dst.at[t, 1], left),
            reduce(6, nb_src.at[t, 0, low], nb_dst.at[t, 0, low], right),
            reduce(7, nb_src.at[t, 1, top], nb_dst.at[t, 1, top], left),
            reduce(8, nb_src.at[t, 0, top], nb_dst.at[t, 0, top], right),
            reduce(9, nb_src.at[t, 1, low], nb_dst.at[t, 1, low], left),
        ]
        for d, b in enumerate((sopp, sright, sleft)):
            sib_src[t, d] = part(b).astype(BF16)
            moves[d].start()
        value = part(opp)
        moves[0].wait_recv()
        opp_src[t] = (value + sib_dst[t, 0].astype(F32)).astype(BF16)
        moves[4].start()
        moves[5].start()
        value = part(right)
        moves[1].wait_recv()
        value = value + sib_dst[t, 1].astype(F32)
        nb_src[t, 0, half:, :] = value[half:].astype(BF16)
        moves[6].start()
        keep[0] = value[0:half]
        value = part(left)
        moves[2].wait_recv()
        value = value + sib_dst[t, 2].astype(F32)
        nb_src[t, 1, 0:half, :] = value[0:half].astype(BF16)
        moves[7].start()
        keep[1] = value[half:]
        sib_src[t, 3] = part(sib).astype(BF16)
        moves[3].start()
        moves[4].wait_recv()
        nb_src[t, 0, 0:half, :] = (keep[0] + rel_dst[t, 0].astype(F32)).astype(BF16)
        moves[8].start()
        moves[5].wait_recv()
        nb_src[t, 1, half:, :] = (keep[1] + rel_dst[t, 1].astype(F32)).astype(BF16)
        moves[9].start()
        value = part(me) + xb[t, me].astype(F32)
        keep[0] = value[0:half]
        keep[1] = value[half:]

        @pl.when((t == 0) & (s < levels))
        def _():
            pltpu.make_async_remote_copy(
                src_ref=fbuf.at[pl.ds(0, (S - 1) * PAD)],
                dst_ref=fbuf.at[pl.ds(0, (S - 1) * PAD)],
                send_sem=fs_sem.at[0],
                recv_sem=fr_sem,
                device_id={"section": 0},
                device_id_type=MESH,
            ).wait_recv()
            for step in range(steps):
                inj[step] = lax.dot_general(
                    fbuf[:, C + step * R : C + (step + 1) * R],
                    fbuf[:, 0:C],
                    (((0,), (0,)), ((), ())),
                    preferred_element_type=F32,
                )

        @pl.when(s < levels)
        def _():
            keep[0] += inj[t, 0:half, :]
            keep[1] += inj[t, half:, :]

        moves[3].wait_recv()
        for h, (a, b) in enumerate(((8, 7), (6, 9))):
            moves[a].wait_recv()
            moves[b].wait_recv()
            these = slice(h * half, (h + 1) * half)
            yb[t, these, :] = (
                keep[h]
                + sib_dst[t, 3, these, :].astype(F32)
                + nb_dst[t, 0, these, :].astype(F32)
                + nb_dst[t, 1, these, :].astype(F32)
            ).astype(BF16)

            @pl.when((t == 0) & (s < S - 1))
            def _():
                shift(yb.at[0], 1, h).start()

        for copy in sends + moves:
            copy.wait_send()
        return carry

    def appended(step):
        return pltpu.make_async_copy(
            kv.at[pl.ds(pl.multiple_of(off + step * R, R), R)],
            kv_out.at[pl.ds(step * R, R)],
            out_sem.at[step],
        )

    lax.fori_loop(0, steps, step_body, 0)
    final = pltpu.make_async_copy(yb.at[steps - 1], out, out_sem.at[steps])
    final.start()
    for step in range(steps):
        appended(step).wait()

    @pl.when(s < S - 1)
    def _():
        for h in range(2):
            shift(pend, 0, h).wait_send()
            shift(yb.at[0], 1, h).wait_send()

    for level in range(levels):

        @pl.when(s != level)
        def _():
            feature(level).wait_send()

    final.wait()


def body(sections, tensors, pend, emb, wq, wkv, wo, memo, in_gain, q_gain, k_gain, feat, pos):
    R, C = pend.shape
    steps = emb.shape[0] // R
    D = C * tensors
    HC = wq.shape[2]
    HD = 128
    rows, levels = feat.shape[0], feat.shape[1]
    cap = memo.shape[1]
    chunk = 4 * R
    slots = -(-(cap + steps * R) // chunk) * chunk
    anyspec = pl.BlockSpec(memory_space=pl.ANY)
    V = pltpu.VMEM
    DMA = pltpu.SemaphoreType.DMA
    hidden, appended = pl.pallas_call(
        functools.partial(kernel, sections),
        out_shape=(
            jax.ShapeDtypeStruct((R, C), BF16),
            jax.ShapeDtypeStruct((steps * R, 2 * HD), BF16),
        ),
        in_specs=[anyspec] * 10 + [pl.BlockSpec(memory_space=pltpu.SMEM)],
        out_specs=(anyspec, anyspec),
        scratch_shapes=[
            V((tensors, C, HC + 2 * HD), BF16),
            V((tensors, HC, C), BF16),
            V((slots, 2 * HD), BF16),
            V((1, D), F32),
            V((1, HD), F32),
            V((1, HD), F32),
            V((rows, levels, C), BF16),
            V((levels, PAD, C + steps * R), BF16),
            V((sections * PAD, C + steps * R), BF16),
            V((steps, R, C), F32),
            V((steps, R, HD), F32),
            V((steps, R, HD), F32),
            V((steps, tensors, R, C), BF16),
            V((R, HD), F32),
            V((R, HC + 2 * HD), F32),
            V((HC // HD * R, HD), BF16),
            V((HC // HD * R, 2 * HD), F32),
            V((R, HC), BF16),
            V((steps, 4, R, C), BF16),
            V((steps, 4, R, C), BF16),
            V((steps, R, C), BF16),
            V((steps, 2, R // 2, C), BF16),
            V((steps, 2, R, C), BF16),
            V((steps, 2, R, C), BF16),
            V((2, R // 2, C), F32),
            V((steps, R, C), BF16),
            DMA((7 + tensors,)),
            DMA((steps,)),
            DMA((levels,)),
            DMA,
            DMA((steps, 16)),
            DMA((steps, 16)),
            DMA((steps, 10)),
            DMA((steps, 10)),
            DMA((steps + 1,)),
        ],
        compiler_params=pltpu.CompilerParams(
            collective_id=0, has_side_effects=True, vmem_limit_bytes=48 * 1024 * 1024
        ),
    )(
        pend,
        emb,
        wq.reshape(tensors, C, HC),
        wkv.reshape(tensors, C, 2 * HD),
        wo.reshape(HC, D),
        memo.reshape(cap, 2 * HD),
        in_gain,
        q_gain,
        k_gain,
        feat,
        pos,
    )
    return hidden, appended.reshape(1, steps * R, 2 * HD)


def solution(mesh):
    return jax.shard_map(
        functools.partial(body, mesh.shape["section"], mesh.shape["tensor"]),
        mesh=mesh,
        in_specs=(
            P("section", "tensor"),
            P(None, "tensor"),
            P("section", None, "tensor"),
            P("section", None, "tensor"),
            P("section", "tensor", None),
            P("section", None, "tensor"),
            P("section", None),
            P("section", None),
            P("section", None),
            P("section", None, "tensor"),
            P("section"),
        ),
        out_specs=(P("section", "tensor"), P("section", None, "tensor")),
        check_vma=False,
    )
```

time: 349 us -> 75 us (0.21)
  waiting for transfers between devices: 243 us -> 0 us
  Pallas kernels: 0 us -> 64.2 us
  blocking collectives: 22.3 us -> 0 us
  local copies, waits for them, and re-layouts: 27.9 us -> 9.8 us
  matrix products: 16.7 us -> 0 us
  other arithmetic: 16.1 us -> 0 us
  between operations: 15 us -> 0.66 us
  starting transfers between devices: 6.76 us -> 0 us
    psum x2 -> x0, waiting for transfers between devices: 136 us -> none  [body(): lax.psum((partial_sum + placed).astype(jnp.bfloat16), 'tensor')]
    all_gather x3 -> x0, waiting for transfers between devices: 82.3 us -> none  [the longest x1 58.2 us: body(): lax.all_gather(deepstack_visual_features, 'section', axis=0, tiled=True)]
    pallas_call x0 -> x1, Pallas kernels: none -> 64.2 us  [body(): pl.pallas_call(functools.partial(kernel, sections), out_shape=(jax.ShapeD...]
    ppermute x2 -> x0, waiting for transfers between devices: 23.3 us -> none  [from_behind(): return lax.ppermute(value, axis, pairs)]
    unnamed x1 -> x0, blocking collectives: 22.3 us -> none
    dot_general x12 -> x0, matrix products: 16.7 us -> none  [the longest x2 6.52 us: attention(): jnp.einsum('ckgh,pkh->kgcp', query, keys, preferred_element_type=jnp.floa...]
    dot_general x1 -> x0, local copies, waits for them, and re-layouts: 6.89 us -> none  [layer_core(): query = jnp.dot(normed, query_w, preferred_element_type=jnp.float32)]
    ppermute x2 -> x0, starting transfers between devices: 6.57 us -> none  [from_behind(): return lax.ppermute(value, axis, pairs)]
  transfers between devices with their start and end apart: 7 -> 0, of which waited for: 5 -> 0; matrix products, arithmetic and copies ran while one was open for 8% -> 0% of each run, Pallas kernels for 0% -> 0%
where the time goes in v1:
time: 75 us; the launch traced here: 74.6 us
  Pallas kernels  64.2 us (86%)
  local copies, waits for them, and re-layouts  9.8 us (13%)
    pallas_call x1, Pallas kernels, body(): pl.pallas_call(functools.partial(kernel, sections), out_shape=(jax.ShapeD...  64.2 us
    unnamed x20, local copies, waits for them, and re-layouts  9.8 us

profile of v1, /device:TPU:8, one launch (start us, length us, event | category | flops | bytes accessed | tf_op | source)
XLA Modules:
  0.0 74.6 jit_solution(10025580792832036233)
XLA Ops:
  0.6 0.0 copy-start
  0.6 1.6 %copy-done = bf16[1,4096,256]{2,1,0:T(8,128)(2,1)S(1)} copy-done((bf16[1,4096,256]{2,1,0:T(8,128)(2,1)S(1)}, bf16[1,4096,256]{2,1,0:T(8,128)(2,1)}, u32[]{:S(2)}) %copy-start) | copy-done | bytes 2097176
  2.2 0.0 copy-start.1
  2.2 1.6 %copy-done.1 = bf16[1,3968,256]{2,1,0:T(8,128)(2,1)S(1)} copy-done((bf16[1,3968,256]{2,1,0:T(8,128)(2,1)S(1)}, bf16[1,3968,256]{2,1,0:T(8,128)(2,1)}, u32[]{:S(2)}) %copy-start.1) | copy-done | bytes 2031640
  3.8 0.0 copy-start.2
  3.8 0.9 %copy-done.2 = bf16[256,512]{1,0:T(8,128)(2,1)S(1)} copy-done((bf16[256,512]{1,0:T(8,128)(2,1)S(1)}, bf16[256,512]{1,0:T(8,128)(2,1)}, u32[]{:S(2)}) %copy-start.2) | copy-done | bytes 262168
  4.7 0.0 copy-start.3
  4.7 0.9 %copy-done.3 = bf16[128,512]{1,0:T(8,128)(2,1)S(1)} copy-done((bf16[128,512]{1,0:T(8,128)(2,1)S(1)}, bf16[128,512]{1,0:T(8,128)(2,1)}, u32[]{:S(2)}) %copy-start.3) | copy-done | bytes 131096
  5.7 0.0 copy-start.4
  5.7 0.8 %copy-done.4 = bf16[12,3,512]{2,1,0:T(4,128)(2,1)S(1)} copy-done((bf16[12,3,512]{2,1,0:T(4,128)(2,1)S(1)}, bf16[12,3,512]{2,1,0:T(4,128)(2,1)}, u32[]{:S(2)}) %copy-start.4) | copy-done | bytes 36888
  6.4 0.0 copy-start.5
  6.5 0.7 copy-done.5
  7.2 0.0 copy-start.6
  7.2 0.7 copy-done.6
  7.8 0.0 copy-start.7
  7.8 0.7 copy-done.7
  8.5 0.0 copy-start.8
  8.5 0.7 copy-done.8
  9.1 64.2 %shard_map.122 = (bf16[128,512]{1,0:T(8,128)(2,1)S(1)}, bf16[256,256]{1,0:T(8,128)(2,1)S(1)}) custom-call(bf16[128,512]{1,0:T(8,128)(2,1)S(1)} %copy-done.3, bf16[256,512]{1,0:T(8,128)(2,1)S(1)} %copy-done.2, bf16[8,512,512]{2,1,0:T(8,128)(2,1)} %bitcast.8, bf16[8,512,256]{2,1,0:T(8,128)(2,1)S(1)} %bitcast.5, bf16[512,4096]{1,0:T(8,128)(2,1)} %bitcast.9, ...), custom_call_target="tpu_custom_call" | custom-call | tf_op jit(solution)/shard_map/pallas_call | solution.py:488
  73.3 0.7 copy.15
  74.0 0.7 copy.16
Async XLA Ops:
  0.6 1.6 %copy-start = (bf16[1,4096,256]{2,1,0:T(8,128)(2,1)S(1)}, bf16[1,4096,256]{2,1,0:T(8,128)(2,1)}, u32[]{:S(2)}) copy-start(bf16[1,4096,256]{2,1,0:T(8,128)(2,1)} %param.14) | copy-start | bytes 6291460
  2.2 1.6 %copy-start.1 = (bf16[1,3968,256]{2,1,0:T(8,128)(2,1)S(1)}, bf16[1,3968,256]{2,1,0:T(8,128)(2,1)}, u32[]{:S(2)}) copy-start(bf16[1,3968,256]{2,1,0:T(8,128)(2,1)} %param.16) | copy-start | bytes 6094852
  3.8 0.9 %copy-start.2 = (bf16[256,512]{1,0:T(8,128)(2,1)S(1)}, bf16[256,512]{1,0:T(8,128)(2,1)}, u32[]{:S(2)}) copy-start(bf16[256,512]{1,0:T(8,128)(2,1)} %emb.1) | copy-start | bytes 786436
  4.7 0.9 %copy-start.3 = (bf16[128,512]{1,0:T(8,128)(2,1)S(1)}, bf16[128,512]{1,0:T(8,128)(2,1)}, u32[]{:S(2)}) copy-start(bf16[128,512]{1,0:T(8,128)(2,1)} %pend.1) | copy-start | bytes 393220
  5.7 0.8 %copy-start.4 = (bf16[12,3,512]{2,1,0:T(4,128)(2,1)S(1)}, bf16[12,3,512]{2,1,0:T(4,128)(2,1)}, u32[]{:S(2)}) copy-start(bf16[12,3,512]{2,1,0:T(4,128)(2,1)} %feat_h.1) | copy-start | bytes 110596
  6.4 0.7 copy-start.5
  7.2 0.7 copy-start.6
  7.8 0.7 copy-start.7
  8.5 0.7 copy-start.8

commit v2 on v1

v2 whole, which is shorter than its diff:
```python
import functools
import math

import jax
import jax.numpy as jnp
from jax import lax
from jax.experimental import pallas as pl
from jax.experimental.pallas import tpu as pltpu
from jax.sharding import PartitionSpec as P

MESH = pl.DeviceIdType.MESH
EPS = 1e-06
THETA = 5000000.0
PAD = 16
F32 = jnp.float32
BF16 = jnp.bfloat16


def kernel(
    sections,
    pend,
    emb,
    wq_h,
    wkv_h,
    wo_h,
    memo,
    in_gain_h,
    q_gain_h,
    k_gain_h,
    feat_h,
    pos,
    out,
    kv_out,
    wqkv,
    wo,
    kv,
    in_gain,
    q_gain,
    k_gain,
    feat,
    msg,
    fbuf,
    inj,
    cs,
    sn,
    xb,
    ss,
    acc,
    qs,
    ps,
    pv,
    att,
    wo_sib,
    nb_src,
    nb_dst,
    keep,
    yb,
    load_sem,
    emb_sem,
    fs_sem,
    fr_sem,
    ags,
    agr,
    rss,
    rsr,
    ws,
    wr,
    out_sem,
):
    S = sections
    steps, T, R, C = xb.shape
    half = R // 2
    HD = 128
    HC = att.shape[3]
    G = HC // HD
    D = T * C
    rows, levels = feat.shape[0], feat.shape[1]
    chunk = 8 * R
    s = lax.axis_index("section")
    me = lax.axis_index("tensor")
    x = me // 2
    c = me % 2
    ring = T // 2

    def block(step, parity):
        return 2 * ((x + step) % ring) + parity

    sib = block(0, 1 - c)
    right, left, opp = block(1, c), block(ring - 1, c), block(2, c)
    sright, sleft, sopp = block(1, 1 - c), block(ring - 1, 1 - c), block(2, 1 - c)
    off = pl.multiple_of((S - 1 - s) * R, R)

    ends = [
        (feat_h, feat),
        (in_gain_h, in_gain),
        (q_gain_h, q_gain),
        (k_gain_h, k_gain),
        (wq_h, wqkv.at[:, :, pl.ds(0, HC)]),
        (wkv_h, wqkv.at[:, :, pl.ds(HC, 2 * HD)]),
        (memo, kv.at[pl.ds(0, memo.shape[0])]),
    ] + [
        (wo_h.at[:, pl.ds(pl.multiple_of((2 * j + c) * C, C), C)], wo.at[j])
        for j in range(ring)
    ]

    def load(i):
        return pltpu.make_async_copy(*ends[i], load_sem.at[i])

    for i in range(7 + ring):
        load(i).start()

    def enter(step):
        return pltpu.make_async_copy(
            emb.at[pl.ds(step * R, R)], xb.at[step, me], emb_sem.at[step]
        )

    @pl.when(s == 0)
    def _():
        for step in range(steps):
            enter(step).start()

    barrier = pltpu.get_barrier_semaphore()
    for peer in (sib, right, left, opp):
        pl.semaphore_signal(barrier, inc=1, device_id={"tensor": peer}, device_id_type=MESH)

    @pl.when(s < levels)
    def _():
        def greet(k, carry):
            @pl.when(k != s)
            def _():
                pl.semaphore_signal(barrier, inc=1, device_id={"section": k}, device_id_type=MESH)

            return carry

        lax.fori_loop(0, S, greet, 0)

    @pl.when(s >= levels)
    def _():
        pl.semaphore_signal(barrier, inc=1, device_id={"section": s - 1}, device_id_type=MESH)

    peers = 4 + levels - jnp.where(s < levels, 1, 0)
    peers = peers + jnp.where((s >= levels - 1) & (s < S - 1), 1, 0)
    pl.semaphore_wait(barrier, peers)

    def shift(source, step, h):
        return pltpu.make_async_remote_copy(
            src_ref=source.at[pl.ds(h * half, half)],
            dst_ref=xb.at[step, me, pl.ds(h * half, half)],
            send_sem=ags.at[step, h],
            recv_sem=agr.at[step, h],
            device_id={"section": jnp.minimum(s + 1, S - 1)},
            device_id_type=MESH,
        )

    @pl.when(s < S - 1)
    def _():
        for h in range(2):
            shift(pend, 0, h).start()

    def weights(j):
        return pltpu.make_async_remote_copy(
            src_ref=wo_h.at[:, pl.ds(pl.multiple_of((2 * j + 1 - c) * C, C), C)],
            dst_ref=wo_sib.at[j],
            send_sem=ws.at[j],
            recv_sem=wr.at[j],
            device_id={"tensor": sib},
            device_id_type=MESH,
        )

    for j in range(ring):
        weights(j).start()

    for i in range(4):
        load(i).wait()
    col = lax.broadcasted_iota(jnp.int32, (PAD, steps * R), 1)
    row = lax.broadcasted_iota(jnp.int32, (PAD, steps * R), 0)
    place = jnp.full((PAD, steps * R), -1000000, jnp.int32)
    for r in range(rows):
        place = jnp.where(row == r, pos[r], place)
    msg[...] = jnp.zeros_like(msg)
    everything = feat[...].astype(F32)
    for level in range(levels):
        msg[level, 0:rows, 0:C] = everything[:, level, :].astype(BF16)
        hit = place - (levels - 1 - level) * R == col
        msg[level, :, C:] = jnp.where(hit, 1.0, 0.0).astype(BF16)

    def feature(level):
        return pltpu.make_async_remote_copy(
            src_ref=msg.at[level],
            dst_ref=fbuf.at[pl.ds(s * PAD, PAD)],
            send_sem=fs_sem.at[level],
            recv_sem=fr_sem,
            device_id={"section": level},
            device_id_type=MESH,
        )

    for level in range(levels):

        @pl.when(s == level)
        def _():
            fbuf[pl.ds(pl.multiple_of(s * PAD, PAD), PAD), :] = msg[level]

    lane = lax.broadcasted_iota(jnp.int32, (R, HD), 1)
    fold = jnp.where(lane < HD // 2, lane, lane - HD // 2).astype(F32)
    frequency = jnp.exp(fold * (-2.0 * math.log(THETA) / HD))
    for step in range(steps):
        place = off + step * R + lax.broadcasted_iota(jnp.int32, (R, HD), 0)
        angle = place.astype(F32) * frequency
        cs[step] = jnp.cos(angle)
        sn[step] = jnp.where(lane < HD // 2, -jnp.sin(angle), jnp.sin(angle))
    tail = kv.shape[0] - memo.shape[0]
    kv[pl.ds(memo.shape[0], tail), :] = jnp.zeros((tail, 2 * HD), BF16)

    def piece(t, b, h):
        return xb.at[t, b, pl.ds(h * half, half)]

    def gather(t, h, k):
        b, peer, slot = (
            (me, opp, 12),
            (me, right, 4),
            (me, left, 6),
            (me, sib, 2),
            (left, sib, 8),
            (right, sib, 10),
            (opp, sib, 14),
        )[k]
        return pltpu.make_async_remote_copy(
            src_ref=piece(t, b, h),
            dst_ref=piece(t, b, h),
            send_sem=ags.at[t, 2 + 7 * h + k],
            recv_sem=agr.at[t, slot + h],
            device_id={"tensor": peer},
            device_id_type=MESH,
        )

    def arrived(t, h, slot, b):
        pltpu.make_async_remote_copy(
            src_ref=piece(t, b, h),
            dst_ref=piece(t, b, h),
            send_sem=ags.at[t, 2],
            recv_sem=agr.at[t, slot + h],
            device_id={"tensor": sib},
            device_id_type=MESH,
        ).wait_recv()

    def project(t, h, b, first=False):
        rows_f = xb[t, b, h * half : (h + 1) * half, :].astype(F32)
        square = rows_f * rows_f
        total = square[:, 0:HD]
        for g in range(1, C // HD):
            total = total + square[:, g * HD : (g + 1) * HD]
        gain = in_gain[:, pl.ds(pl.multiple_of(b * C, C), C)]
        product = jnp.dot((rows_f * gain).astype(BF16), wqkv[b], preferred_element_type=F32)
        if first:
            ss[h] = total
            acc[h] = product
        else:
            ss[h] += total
            acc[h] += product

    def start(t, h):
        @pl.when(s > 0)
        def _():
            arrived(t, h, 0, me)

        if h == 0:

            @pl.when(s == 0)
            def _():
                enter(t).wait()

        for k in range(4):
            gather(t, h, k).start()

    def forward(t, h, which):
        slot, b, k = ((4, left, 4), (6, right, 5), (12, opp, 6))[which]
        arrived(t, h, slot, b)
        gather(t, h, k).start()

    def appended(step):
        return pltpu.make_async_copy(
            kv.at[pl.ds(pl.multiple_of(off + step * R, R), R)],
            kv_out.at[pl.ds(step * R, R)],
            out_sem.at[step],
        )

    def attention(t, h):
        scale = lax.rsqrt(jnp.sum(ss[h], axis=-1, keepdims=True) * (1.0 / D) + EPS)
        cos = cs[t, h * half : (h + 1) * half, :]
        sin = sn[t, h * half : (h + 1) * half, :]

        def head(value, gain):
            value = value * scale
            mean = jnp.sum(value * value, axis=-1, keepdims=True) * (1.0 / HD)
            value = value * lax.rsqrt(mean + EPS) * gain
            return value * cos + pltpu.roll(value, HD // 2, 1) * sin

        for g in range(G):
            query = head(acc[h, :, g * HD : (g + 1) * HD], q_gain[...])
            qs[g * half : (g + 1) * half, :] = (query * (math.log2(math.e) * HD**-0.5)).astype(BF16)

        if h == 0:

            @pl.when(t == 0)
            def _():
                load(6).wait()

        here = pl.ds(pl.multiple_of(off + t * R + h * half, half), half)
        kv[here, 0:HD] = head(acc[h, :, HC : HC + HD], k_gain[...]).astype(BF16)
        kv[here, HD:] = (acc[h, :, HC + HD :] * scale).astype(BF16)
        if h == 1:
            appended(t).start()

        whole = (off + t * R) // chunk

        def block_of(at):
            return pl.ds(pl.multiple_of(at * chunk, chunk), chunk)

        def score(at):
            return jnp.exp2(
                lax.dot_general(
                    qs[...],
                    kv[block_of(at), 0:HD],
                    (((1,), (1,)), ((), ())),
                    preferred_element_type=F32,
                )
            )

        def weigh(at, place):
            values = jnp.concatenate([kv[block_of(at), HD:], jnp.ones((chunk, HD), BF16)], axis=1)
            pv[...] += jnp.dot(ps[place], values, preferred_element_type=F32)

        pv[...] = jnp.zeros_like(pv)
        slot = whole * chunk + lax.broadcasted_iota(jnp.int32, (half, chunk), 1)
        last = off + t * R + h * half + lax.broadcasted_iota(jnp.int32, (half, chunk), 0)
        weight = jnp.where((slot <= last)[None], score(whole).reshape(G, half, chunk), 0.0)
        ps[0] = weight.reshape(G * half, chunk).astype(BF16)

        def pair(i, carry):
            ps[1] = score(2 * i).astype(BF16)
            weigh(jnp.where(i == 0, whole, 2 * i - 1), 0)
            ps[0] = score(2 * i + 1).astype(BF16)
            weigh(2 * i, 1)
            return carry

        lax.fori_loop(0, whole // 2, pair, 0)
        left_over = jnp.where(whole < 2, whole, 2 * (whole // 2) - 1)

        @pl.when(whole % 2 == 1)
        def _():
            ps[1] = score(whole - 1).astype(BF16)
            weigh(left_over, 0)
            weigh(whole - 1, 1)

        @pl.when(whole % 2 == 0)
        def _():
            weigh(left_over, 0)

        for g in range(G):
            found = pv[g * half : (g + 1) * half, :]
            att[t, 0, h * half : (h + 1) * half, g * HD : (g + 1) * HD] = (
                found[:, 0:HD] / found[:, HD:]
            ).astype(BF16)
        reduce(t, h, 0).start()

    def reduce(t, h, k):
        these = pl.ds(h * half, half)
        if k == 0:
            source, target = att.at[t, 0, these], att.at[t, 1, these]
        else:
            source, target = nb_src.at[t, k - 1, these], nb_dst.at[t, k - 1, these]
        return pltpu.make_async_remote_copy(
            src_ref=source,
            dst_ref=target,
            send_sem=rss.at[t, 4 * h + k],
            recv_sem=rsr.at[t, 4 * h + k],
            device_id={"tensor": (sib, opp, right, left)[k]},
            device_id_type=MESH,
        )

    def part(t, h, b, heads, table):
        return jnp.dot(
            att[t, heads, h * half : (h + 1) * half, :], table[b], preferred_element_type=F32
        )

    def own_part(t, h):
        if h == 0:

            @pl.when(t == 0)
            def _():
                for j in range(ring):
                    load(7 + j).wait()
                    weights(j).wait_recv()

        for d, b in enumerate((opp, right, left, me)):
            keep[h, d] = part(t, h, b // 2, 0, wo)

    def other_part(t, h):
        these = slice(h * half, (h + 1) * half)
        reduce(t, h, 0).wait_recv()
        for d, b in enumerate((opp, right, left)):
            nb_src[t, d, these, :] = (keep[h, d] + part(t, h, b // 2, 1, wo_sib)).astype(BF16)
            reduce(t, h, 1 + d).start()
        keep[h, 3] += part(t, h, x, 1, wo_sib) + xb[t, me, these, :].astype(F32)

    def inject():
        pltpu.make_async_remote_copy(
            src_ref=fbuf.at[pl.ds(0, (S - 1) * PAD)],
            dst_ref=fbuf.at[pl.ds(0, (S - 1) * PAD)],
            send_sem=fs_sem.at[0],
            recv_sem=fr_sem,
            device_id={"section": 0},
            device_id_type=MESH,
        ).wait_recv()
        for step in range(steps):
            inj[step] = lax.dot_general(
                fbuf[:, C + step * R : C + (step + 1) * R],
                fbuf[:, 0:C],
                (((0,), (0,)), ((), ())),
                preferred_element_type=F32,
            )

    def finish(t, h):
        these = slice(h * half, (h + 1) * half)

        @pl.when(s < levels)
        def _():
            keep[h, 3] += inj[t, these, :]

        total = keep[h, 3]
        for d in (1, 2, 0):
            reduce(t, h, 1 + d).wait_recv()
            total = total + nb_dst[t, d, these, :].astype(F32)
        yb[t, these, :] = total.astype(BF16)

        @pl.when((t == 0) & (s < S - 1))
        def _():
            shift(yb.at[0], 1, h).start()

    def step_body(t, carry):
        @pl.when(t > 0)
        def _():
            finish(jnp.maximum(t - 1, 0), 1)

        @pl.when(t == 0)
        def _():
            for i in (4, 5):
                load(i).wait()

        project(t, 0, me, True)
        arrived(t, 0, 2, sib)
        project(t, 0, sib)
        forward(t, 0, 0)
        forward(t, 0, 1)
        project(t, 0, left)
        forward(t, 0, 2)
        project(t, 0, right)

        @pl.when(t > 0)
        def _():
            start(t, 1)

        project(t, 0, opp)
        arrived(t, 0, 8, sleft)
        project(t, 0, sleft)
        arrived(t, 0, 10, sright)
        project(t, 0, sright)
        arrived(t, 0, 14, sopp)
        project(t, 0, sopp)

        @pl.when(t == 0)
        def _():
            for which in range(3):
                forward(t, 1, which)

        attention(t, 0)
        own_part(t, 0)
        other_part(t, 0)

        @pl.when(t > 0)
        def _():
            for which in range(3):
                forward(t, 1, which)

        project(t, 1, me, True)
        project(t, 1, left)
        project(t, 1, right)
        project(t, 1, opp)
        for slot, b in ((2, sib), (8, sleft), (10, sright), (14, sopp)):
            arrived(t, 1, slot, b)
            project(t, 1, b)
        attention(t, 1)
        own_part(t, 1)

        @pl.when((t == 0) & (s < levels))
        def _():
            inject()

        finish(t, 0)
        other_part(t, 1)

        @pl.when(t + 1 < steps)
        def _():
            start(jnp.minimum(t + 1, steps - 1), 0)

        return carry

    start(0, 0)
    start(0, 1)
    for level in range(levels):

        @pl.when(s != level)
        def _():
            feature(level).start()

    lax.fori_loop(0, steps, step_body, 0)

    def sent(t, carry):
        for h in range(2):
            for k in range(7):
                gather(t, h, k).wait_send()
            for k in range(4):
                reduce(t, h, k).wait_send()
        return carry

    lax.fori_loop(0, steps - 1, sent, 0)

    @pl.when(s < S - 1)
    def _():
        for h in range(2):
            shift(pend, 0, h).wait_send()
            shift(yb.at[0], 1, h).wait_send()

    for j in range(ring):
        weights(j).wait_send()

    for level in range(levels):

        @pl.when(s != level)
        def _():
            feature(level).wait_send()

    finish(steps - 1, 1)
    final = pltpu.make_async_copy(yb.at[steps - 1], out, out_sem.at[steps])
    final.start()
    sent(steps - 1, 0)
    for step in range(steps):
        appended(step).wait()
    final.wait()


def deliver(hidden, appended, hidden_out, appended_out, held, kept, in_sem, out_sem):
    ways = [(hidden, held, hidden_out), (appended, kept, appended_out)]
    for i, (source, between, target) in enumerate(ways):
        pltpu.make_async_copy(source, between, in_sem.at[i]).start()
    for i, (source, between, target) in enumerate(ways):
        pltpu.make_async_copy(source, between, in_sem.at[i]).wait()
        pltpu.make_async_copy(between, target, out_sem.at[i]).start()
    for i, (source, between, target) in enumerate(ways):
        pltpu.make_async_copy(between, target, out_sem.at[i]).wait()


def body(sections, tensors, pend, emb, wq, wkv, wo, memo, in_gain, q_gain, k_gain, feat, pos):
    R, C = pend.shape
    steps = emb.shape[0] // R
    D = C * tensors
    HC = wq.shape[2]
    HD = 128
    rows, levels = feat.shape[0], feat.shape[1]
    cap = memo.shape[1]
    chunk = 8 * R
    slots = -(-(cap + steps * R) // chunk) * chunk
    anyspec = pl.BlockSpec(memory_space=pl.ANY)
    V = pltpu.VMEM
    DMA = pltpu.SemaphoreType.DMA
    hidden, appended = pl.pallas_call(
        functools.partial(kernel, sections),
        out_shape=(
            jax.ShapeDtypeStruct((R, C), BF16),
            jax.ShapeDtypeStruct((steps * R, 2 * HD), BF16),
        ),
        in_specs=[anyspec] * 10 + [pl.BlockSpec(memory_space=pltpu.SMEM)],
        out_specs=(anyspec, anyspec),
        scratch_shapes=[
            V((tensors, C, HC + 2 * HD), BF16),
            V((tensors // 2, HC, C), BF16),
            V((slots, 2 * HD), BF16),
            V((1, D), F32),
            V((1, HD), F32),
            V((1, HD), F32),
            V((rows, levels, C), BF16),
            V((levels, PAD, C + steps * R), BF16),
            V((sections * PAD, C + steps * R), BF16),
            V((steps, R, C), F32),
            V((steps, R, HD), F32),
            V((steps, R, HD), F32),
            V((steps, tensors, R, C), BF16),
            V((2, R // 2, HD), F32),
            V((2, R // 2, HC + 2 * HD), F32),
            V((HC // HD * R // 2, HD), BF16),
            V((2, HC // HD * R // 2, chunk), BF16),
            V((HC // HD * R // 2, 2 * HD), F32),
            V((steps, 2, R, HC), BF16),
            V((tensors // 2, HC, C), BF16),
            V((steps, 3, R, C), BF16),
            V((steps, 3, R, C), BF16),
            V((2, 4, R // 2, C), F32),
            V((steps, R, C), BF16),
            DMA((7 + tensors // 2,)),
            DMA((steps,)),
            DMA((levels,)),
            DMA,
            DMA((steps, 16)),
            DMA((steps, 16)),
            DMA((steps, 8)),
            DMA((steps, 8)),
            DMA((tensors // 2,)),
            DMA((tensors // 2,)),
            DMA((steps + 1,)),
        ],
        compiler_params=pltpu.CompilerParams(
            collective_id=0, has_side_effects=True, vmem_limit_bytes=64 * 1024 * 1024
        ),
    )(
        pend,
        emb,
        wq.reshape(tensors, C, HC),
        wkv.reshape(tensors, C, 2 * HD),
        wo.reshape(HC, D),
        memo.reshape(cap, 2 * HD),
        in_gain,
        q_gain,
        k_gain,
        feat,
        pos,
    )
    hidden, appended = pl.pallas_call(
        deliver,
        out_shape=(
            jax.ShapeDtypeStruct((R, C), BF16),
            jax.ShapeDtypeStruct((steps * R, 2 * HD), BF16),
        ),
        in_specs=[anyspec] * 2,
        out_specs=(anyspec, anyspec),
        scratch_shapes=[V((R, C), BF16), V((steps * R, 2 * HD), BF16), DMA((2,)), DMA((2,))],
        compiler_params=pltpu.CompilerParams(vmem_limit_bytes=64 * 1024 * 1024),
    )(hidden, appended)
    return hidden, appended.reshape(1, steps * R, 2 * HD)


def solution(mesh):
    return jax.shard_map(
        functools.partial(body, mesh.shape["section"], mesh.shape["tensor"]),
        mesh=mesh,
        in_specs=(
            P("section", "tensor"),
            P(None, "tensor"),
            P("section", None, "tensor"),
            P("section", None, "tensor"),
            P("section", "tensor", None),
            P("section", None, "tensor"),
            P("section", None),
            P("section", None),
            P("section", None),
            P("section", None, "tensor"),
            P("section"),
        ),
        out_specs=(P("section", "tensor"), P("section", None, "tensor")),
        check_vma=False,
    )
```

time: 75 us -> 56.8 us (0.76)
  local copies, waits for them, and re-layouts: 9.8 us -> 0 us
  Pallas kernels: 64.2 us -> 55.8 us
    pallas_call x1, Pallas kernels: 64.2 us -> 54.1 us  [body(): pl.pallas_call(functools.partial(kernel, sections), out_shape=(jax.ShapeD...]
    unnamed x20 -> x0, local copies, waits for them, and re-layouts: 9.8 us -> none
    pallas_call x0 -> x1, Pallas kernels: none -> 1.66 us  [body(): pl.pallas_call(deliver, out_shape=(jax.ShapeDtypeStruct((R, C), BF16), ja...]
where the time goes in v2:
time: 56.8 us; the launch traced here: 56.4 us
  Pallas kernels  55.8 us (98%)
  between operations  0.64 us (1%)
    pallas_call x1, Pallas kernels, body(): pl.pallas_call(functools.partial(kernel, sections), out_shape=(jax.ShapeD...  54.1 us
    pallas_call x1, Pallas kernels, body(): pl.pallas_call(deliver, out_shape=(jax.ShapeDtypeStruct((R, C), BF16), ja...  1.66 us

profile of v2, /device:TPU:8, one launch (start us, length us, event | category | flops | bytes accessed | tf_op | source)
XLA Modules:
  0.0 56.4 jit_solution(817269287604541579)
XLA Ops:
  0.6 54.1 %shard_map.122 = (bf16[128,512]{1,0:T(8,128)(2,1)}, bf16[256,256]{1,0:T(8,128)(2,1)}) custom-call(bf16[128,512]{1,0:T(8,128)(2,1)} %pend.1, bf16[256,512]{1,0:T(8,128)(2,1)} %emb.1, bf16[8,512,512]{2,1,0:T(8,128)(2,1)} %bitcast.5, bf16[8,512,256]{2,1,0:T(8,128)(2,1)} %bitcast.7, bf16[512,4096]{1,0:T(8,128)(2,1)} %bitcast.6, bf16[3968,256]{1,0:T(8,128)(2,1)} %bitcast.8, ...), custom_call_target="tpu_custom_call" | custom-call | tf_op jit(solution)/shard_map/pallas_call | solution.py:576
  54.8 1.7 %shard_map.123 = (bf16[128,512]{1,0:T(8,128)(2,1)}, bf16[256,256]{1,0:T(8,128)(2,1)}) custom-call(bf16[128,512]{1,0:T(8,128)(2,1)} %get-tuple-element.6.hidden, bf16[256,256]{1,0:T(8,128)(2,1)} %get-tuple-element.7.appended), custom_call_target="tpu_custom_call" | custom-call | tf_op jit(solution)/shard_map/pallas_call | solution.py:637

commit v3 on v2

--- a/solution.py
+++ b/solution.py
@@ -31,6 +31,7 @@
     pos,
     out,
     kv_out,
+    pend_v,
     wqkv,
     wo,
     kv,
@@ -90,7 +91,27 @@
     sright, sleft, sopp = block(1, 1 - c), block(ring - 1, 1 - c), block(2, 1 - c)
     off = pl.multiple_of((S - 1 - s) * R, R)
 
+    barrier = pltpu.get_barrier_semaphore()
+    for peer in (sib, right, left, opp):
+        pl.semaphore_signal(barrier, inc=1, device_id={"tensor": peer}, device_id_type=MESH)
+
+    @pl.when(s < levels)
+    def _():
+        def greet(k, carry):
+            @pl.when(k != s)
+            def _():
+                pl.semaphore_signal(barrier, inc=1, device_id={"section": k}, device_id_type=MESH)
+
+            return carry
+
+        lax.fori_loop(0, S, greet, 0)
+
+    @pl.when(s >= levels)
+    def _():
+        pl.semaphore_signal(barrier, inc=1, device_id={"section": s - 1}, device_id_type=MESH)
+
     ends = [
+        (pend, pend_v),
         (feat_h, feat),
         (in_gain_h, in_gain),
         (q_gain_h, q_gain),
@@ -106,7 +127,7 @@
     def load(i):
         return pltpu.make_async_copy(*ends[i], load_sem.at[i])
 
-    for i in range(7 + ring):
+    for i in range(8 + ring):
         load(i).start()
 
     def enter(step):
@@ -118,25 +139,6 @@
     def _():
         for step in range(steps):
             enter(step).start()
-
-    barrier = pltpu.get_barrier_semaphore()
-    for peer in (sib, right, left, opp):
-        pl.semaphore_signal(barrier, inc=1, device_id={"tensor": peer}, device_id_type=MESH)
-
-    @pl.when(s < levels)
-    def _():
-        def greet(k, carry):
-            @pl.when(k != s)
-            def _():
-                pl.semaphore_signal(barrier, inc=1, device_id={"section": k}, device_id_type=MESH)
-
-            return carry
-
-        lax.fori_loop(0, S, greet, 0)
-
-    @pl.when(s >= levels)
-    def _():
-        pl.semaphore_signal(barrier, inc=1, device_id={"section": s - 1}, device_id_type=MESH)
 
     peers = 4 + levels - jnp.where(s < levels, 1, 0)
     peers = peers + jnp.where((s >= levels - 1) & (s < S - 1), 1, 0)
@@ -152,10 +154,12 @@
             device_id_type=MESH,
         )
 
+    load(0).wait()
+
     @pl.when(s < S - 1)
     def _():
         for h in range(2):
-            shift(pend, 0, h).start()
+            shift(pend_v, 0, h).start()
 
     def weights(j):
         return pltpu.make_async_remote_copy(
@@ -170,7 +174,7 @@
     for j in range(ring):
         weights(j).start()
 
-    for i in range(4):
+    for i in range(1, 5):
         load(i).wait()
     col = lax.broadcasted_iota(jnp.int32, (PAD, steps * R), 1)
     row = lax.broadcasted_iota(jnp.int32, (PAD, steps * R), 0)
@@ -243,20 +247,22 @@
             device_id_type=MESH,
         ).wait_recv()
 
-    def project(t, h, b, first=False):
-        rows_f = xb[t, b, h * half : (h + 1) * half, :].astype(F32)
+    def project(t, halves, b, first=False):
+        rows_f = xb[t, b, halves[0] * half : (halves[-1] + 1) * half, :].astype(F32)
         square = rows_f * rows_f
         total = square[:, 0:HD]
         for g in range(1, C // HD):
             total = total + square[:, g * HD : (g + 1) * HD]
         gain = in_gain[:, pl.ds(pl.multiple_of(b * C, C), C)]
         product = jnp.dot((rows_f * gain).astype(BF16), wqkv[b], preferred_element_type=F32)
-        if first:
-            ss[h] = total
-            acc[h] = product
-        else:
-            ss[h] += total
-            acc[h] += product
+        for i, h in enumerate(halves):
+            these = slice(i * half, (i + 1) * half)
+            if first:
+                ss[h] = total[these]
+                acc[h] = product[these]
+            else:
+                ss[h] += total[these]
+                acc[h] += product[these]
 
     def start(t, h):
         @pl.when(s > 0)
@@ -284,7 +290,7 @@
             out_sem.at[step],
         )
 
-    def attention(t, h):
+    def heads(t, h):
         scale = lax.rsqrt(jnp.sum(ss[h], axis=-1, keepdims=True) * (1.0 / D) + EPS)
         cos = cs[t, h * half : (h + 1) * half, :]
         sin = sn[t, h * half : (h + 1) * half, :]
@@ -299,11 +305,8 @@
             query = head(acc[h, :, g * HD : (g + 1) * HD], q_gain[...])
             qs[g * half : (g + 1) * half, :] = (query * (math.log2(math.e) * HD**-0.5)).astype(BF16)
 
-        if h == 0:
-
-            @pl.when(t == 0)
-            def _():
-                load(6).wait()
+        if h == 0 and t == 0:
+            load(7).wait()
 
         here = pl.ds(pl.multiple_of(off + t * R + h * half, half), half)
         kv[here, 0:HD] = head(acc[h, :, HC : HC + HD], k_gain[...]).astype(BF16)
@@ -311,6 +314,7 @@
         if h == 1:
             appended(t).start()
 
+    def attend(t, h):
         whole = (off + t * R) // chunk
 
         def block_of(at):
@@ -384,13 +388,10 @@
         )
 
     def own_part(t, h):
-        if h == 0:
-
-            @pl.when(t == 0)
-            def _():
-                for j in range(ring):
-                    load(7 + j).wait()
-                    weights(j).wait_recv()
+        if h == 0 and t == 0:
+            for j in range(ring):
+                load(8 + j).wait()
+                weights(j).wait_recv()
 
         for d, b in enumerate((opp, right, left, me)):
             keep[h, d] = part(t, h, b // 2, 0, wo)
@@ -433,87 +434,88 @@
             total = total + nb_dst[t, d, these, :].astype(F32)
         yb[t, these, :] = total.astype(BF16)
 
-        @pl.when((t == 0) & (s < S - 1))
-        def _():
-            shift(yb.at[0], 1, h).start()
-
-    def step_body(t, carry):
-        @pl.when(t > 0)
-        def _():
-            finish(jnp.maximum(t - 1, 0), 1)
-
-        @pl.when(t == 0)
-        def _():
-            for i in (4, 5):
-                load(i).wait()
-
-        project(t, 0, me, True)
-        arrived(t, 0, 2, sib)
-        project(t, 0, sib)
-        forward(t, 0, 0)
-        forward(t, 0, 1)
-        project(t, 0, left)
-        forward(t, 0, 2)
-        project(t, 0, right)
-
-        @pl.when(t > 0)
-        def _():
-            start(t, 1)
-
-        project(t, 0, opp)
-        arrived(t, 0, 8, sleft)
-        project(t, 0, sleft)
-        arrived(t, 0, 10, sright)
-        project(t, 0, sright)
-        arrived(t, 0, 14, sopp)
-        project(t, 0, sopp)
-
-        @pl.when(t == 0)
-        def _():
-            for which in range(3):
-                forward(t, 1, which)
-
-        attention(t, 0)
-        own_part(t, 0)
-        other_part(t, 0)
-
-        @pl.when(t > 0)
-        def _():
-            for which in range(3):
-                forward(t, 1, which)
-
-        project(t, 1, me, True)
-        project(t, 1, left)
-        project(t, 1, right)
-        project(t, 1, opp)
-        for slot, b in ((2, sib), (8, sleft), (10, sright), (14, sopp)):
-            arrived(t, 1, slot, b)
-            project(t, 1, b)
-        attention(t, 1)
-        own_part(t, 1)
-
-        @pl.when((t == 0) & (s < levels))
-        def _():
-            inject()
-
-        finish(t, 0)
-        other_part(t, 1)
-
-        @pl.when(t + 1 < steps)
-        def _():
-            start(jnp.minimum(t + 1, steps - 1), 0)
-
-        return carry
-
-    start(0, 0)
-    start(0, 1)
+        if t + 1 < steps:
+
+            @pl.when(s < S - 1)
+            def _():
+                shift(yb.at[t], t + 1, h).start()
+
+    both = (0, 1)
+    for h in both:
+        start(0, h)
     for level in range(levels):
 
         @pl.when(s != level)
         def _():
             feature(level).start()
 
-    lax.fori_loop(0, steps, step_body, 0)
+    for i in (5, 6):
+        load(i).wait()
+    project(0, both, me, True)
+    for h in both:
+        arrived(0, h, 2, sib)
+    project(0, both, sib)
+    for h in both:
+        forward(0, h, 0)
+        forward(0, h, 1)
+    project(0, both, left)
+    for h in both:
+        forward(0, h, 2)
+    project(0, both, right)
+    project(0, both, opp)
+    for slot, b in ((8, sleft), (10, sright), (14, sopp)):
+        for h in both:
+            arrived(0, h, slot, b)
+        project(0, both, b)
+    heads(0, 0)
+    attend(0, 0)
+    own_part(0, 0)
+    heads(0, 1)
+    other_part(0, 0)
+    attend(0, 1)
+    own_part(0, 1)
+
+    @pl.when(s < levels)
+    def _():
+        inject()
+
+    other_part(0, 1)
+    finish(0, 0)
+
+    for t in range(1, steps):
+        start(t, 0)
+        finish(t - 1, 1)
+        project(t, (0,), me, True)
+        arrived(t, 0, 2, sib)
+        project(t, (0,), sib)
+        start(t, 1)
+        forward(t, 0, 0)
+        forward(t, 0, 1)
+        project(t, (0,), left)
+        forward(t, 0, 2)
+        project(t, (0,), right)
+        project(t, (0,), opp)
+        for slot, b in ((8, sleft), (10, sright), (14, sopp)):
+            arrived(t, 0, slot, b)
+            project(t, (0,), b)
+        heads(t, 0)
+        attend(t, 0)
+        for which in range(3):
+            forward(t, 1, which)
+        own_part(t, 0)
+        project(t, (1,), me, True)
+        project(t, (1,), left)
+        other_part(t, 0)
+        project(t, (1,), right)
+        project(t, (1,), opp)
+        for slot, b in ((2, sib), (8, sleft), (10, sright), (14, sopp)):
+            arrived(t, 1, slot, b)
+            project(t, (1,), b)
+        heads(t, 1)
+        attend(t, 1)
+        own_part(t, 1)
+        other_part(t, 1)
+        finish(t, 0)
 
     def sent(t, carry):
         for h in range(2):
@@ -528,7 +530,7 @@
     @pl.when(s < S - 1)
     def _():
         for h in range(2):
-            shift(pend, 0, h).wait_send()
+            shift(pend_v, 0, h).wait_send()
             shift(yb.at[0], 1, h).wait_send()
 
     for j in range(ring):
@@ -540,13 +542,20 @@
         def _():
             feature(level).wait_send()
 
-    finish(steps - 1, 1)
-    final = pltpu.make_async_copy(yb.at[steps - 1], out, out_sem.at[steps])
-    final.start()
+    def final(h):
+        these = pl.ds(h * half, half)
+        return pltpu.make_async_copy(
+            yb.at[steps - 1, these], out.at[these], out_sem.at[steps + h]
+        )
+
+    final(0).start()
     sent(steps - 1, 0)
     for step in range(steps):
         appended(step).wait()
-    final.wait()
+    finish(steps - 1, 1)
+    final(1).start()
+    for h in both:
+        final(h).wait()
 
 
 def deliver(hidden, appended, hidden_out, appended_out, held, kept, in_sem, out_sem):
@@ -582,6 +591,7 @@
         in_specs=[anyspec] * 10 + [pl.BlockSpec(memory_space=pltpu.SMEM)],
         out_specs=(anyspec, anyspec),
         scratch_shapes=[
+            V((R, C), BF16),
             V((tensors, C, HC + 2 * HD), BF16),
             V((tensors // 2, HC, C), BF16),
             V((slots, 2 * HD), BF16),
@@ -606,7 +616,7 @@
             V((steps, 3, R, C), BF16),
             V((2, 4, R // 2, C), F32),
             V((steps, R, C), BF16),
-            DMA((7 + tensors // 2,)),
+            DMA((8 + tensors // 2,)),
             DMA((steps,)),
             DMA((levels,)),
             DMA,
@@ -616,7 +626,7 @@
             DMA((steps, 8)),
             DMA((tensors // 2,)),
             DMA((tensors // 2,)),
-            DMA((steps + 1,)),
+            DMA((steps + 2,)),
         ],
         compiler_params=pltpu.CompilerParams(
             collective_id=0, has_side_effects=True, vmem_limit_bytes=64 * 1024 * 1024

time: 56.8 us -> 56 us (0.986)
  Pallas kernels: 55.8 us -> 54.8 us
    pallas_call x1, Pallas kernels: 54.1 us -> 53.2 us  [body(): pl.pallas_call(functools.partial(kernel, sections), out_shape=(jax.ShapeD...]
where the time goes in v3:
time: 56 us; the launch traced here: 55.6 us
  Pallas kernels  54.8 us (98%)
  between operations  0.8 us (1%)
    pallas_call x1, Pallas kernels, body(): pl.pallas_call(functools.partial(kernel, sections), out_shape=(jax.ShapeD...  53.2 us
    pallas_call x1, Pallas kernels, body(): pl.pallas_call(deliver, out_shape=(jax.ShapeDtypeStruct((R, C), BF16), ja...  1.66 us

profile of v3, /device:TPU:8, one launch (start us, length us, event | category | flops | bytes accessed | tf_op | source)
XLA Modules:
  0.0 55.6 jit_solution(6882263686741371521)
XLA Ops:
  0.6 53.2 %shard_map.122 = (bf16[128,512]{1,0:T(8,128)(2,1)}, bf16[256,256]{1,0:T(8,128)(2,1)}) custom-call(bf16[128,512]{1,0:T(8,128)(2,1)} %pend.1, bf16[256,512]{1,0:T(8,128)(2,1)} %emb.1, bf16[8,512,512]{2,1,0:T(8,128)(2,1)} %bitcast.5, bf16[8,512,256]{2,1,0:T(8,128)(2,1)} %bitcast.7, bf16[512,4096]{1,0:T(8,128)(2,1)} %bitcast.6, bf16[3968,256]{1,0:T(8,128)(2,1)} %bitcast.8, ...), custom_call_target="tpu_custom_call" | custom-call | tf_op jit(solution)/shard_map/pallas_call | solution.py:585
  53.8 1.7 %shard_map.123 = (bf16[128,512]{1,0:T(8,128)(2,1)}, bf16[256,256]{1,0:T(8,128)(2,1)}) custom-call(bf16[128,512]{1,0:T(8,128)(2,1)} %get-tuple-element.6.hidden, bf16[256,256]{1,0:T(8,128)(2,1)} %get-tuple-element.7.appended), custom_call_target="tpu_custom_call" | custom-call | tf_op jit(solution)/shard_map/pallas_call | solution.py:647

commit v4 on v3

--- a/solution.py
+++ b/solution.py
@@ -335,10 +335,31 @@
             pv[...] += jnp.dot(ps[place], values, preferred_element_type=F32)
 
         pv[...] = jnp.zeros_like(pv)
-        slot = whole * chunk + lax.broadcasted_iota(jnp.int32, (half, chunk), 1)
-        last = off + t * R + h * half + lax.broadcasted_iota(jnp.int32, (half, chunk), 0)
-        weight = jnp.where((slot <= last)[None], score(whole).reshape(G, half, chunk), 0.0)
-        ps[0] = weight.reshape(G * half, chunk).astype(BF16)
+        def masked(width):
+            base = pl.multiple_of(whole * chunk, chunk)
+            value = jnp.exp2(
+                lax.dot_general(
+                    qs[...],
+                    kv[pl.ds(base, width), 0:HD],
+                    (((1,), (1,)), ((), ())),
+                    preferred_element_type=F32,
+                )
+            )
+            slot = base + lax.broadcasted_iota(jnp.int32, (half, width), 1)
+            last = off + t * R + h * half + lax.broadcasted_iota(jnp.int32, (half, width), 0)
+            weight = jnp.where((slot <= last)[None], value.reshape(G, half, width), 0.0)
+            ps[0, :, 0:width] = weight.reshape(G * half, width).astype(BF16)
+
+        few = (off + t * R) % chunk <= R
+
+        @pl.when(few)
+        def _():
+            masked(2 * R)
+            ps[0, :, 2 * R :] = jnp.zeros((G * half, chunk - 2 * R), BF16)
+
+        @pl.when(jnp.logical_not(few))
+        def _():
+            masked(chunk)
 
         def pair(i, carry):
             ps[1] = score(2 * i).astype(BF16)

time: 56 us -> 55.5 us (level)
  no operation moved by 1% of the time
where the time goes in v4:
time: 55.5 us; the launch traced here: 55.1 us
  Pallas kernels  54.3 us (98%)
  between operations  0.8 us (1%)
    pallas_call x1, Pallas kernels, body(): pl.pallas_call(functools.partial(kernel, sections), out_shape=(jax.ShapeD...  52.6 us
    pallas_call x1, Pallas kernels, body(): pl.pallas_call(deliver, out_shape=(jax.ShapeDtypeStruct((R, C), BF16), ja...  1.66 us

profile of v4, /device:TPU:8, one launch (start us, length us, event | category | flops | bytes accessed | tf_op | source)
XLA Modules:
  0.0 55.1 jit_solution(8658901518881050672)
XLA Ops:
  0.6 52.6 %shard_map.122 = (bf16[128,512]{1,0:T(8,128)(2,1)}, bf16[256,256]{1,0:T(8,128)(2,1)}) custom-call(bf16[128,512]{1,0:T(8,128)(2,1)} %pend.1, bf16[256,512]{1,0:T(8,128)(2,1)} %emb.1, bf16[8,512,512]{2,1,0:T(8,128)(2,1)} %bitcast.5, bf16[8,512,256]{2,1,0:T(8,128)(2,1)} %bitcast.7, bf16[512,4096]{1,0:T(8,128)(2,1)} %bitcast.6, bf16[3968,256]{1,0:T(8,128)(2,1)} %bitcast.8, ...), custom_call_target="tpu_custom_call" | custom-call | tf_op jit(solution)/shard_map/pallas_call | solution.py:606
  53.3 1.7 %shard_map.123 = (bf16[128,512]{1,0:T(8,128)(2,1)}, bf16[256,256]{1,0:T(8,128)(2,1)}) custom-call(bf16[128,512]{1,0:T(8,128)(2,1)} %get-tuple-element.6.hidden, bf16[256,256]{1,0:T(8,128)(2,1)} %get-tuple-element.7.appended), custom_call_target="tpu_custom_call" | custom-call | tf_op jit(solution)/shard_map/pallas_call | solution.py:668
